TPU v7x, 32 devices: a whole 2x2x4 slice. The times are simulated.
32 devices in a mesh: sig: 16 (over z, y, x), xf: 2 (over core).
Axes of the slice: x: 2, y: 2, z: 4, core: 2. Of those that a mesh axis runs over, the one named last changes fastest.
Arguments:
- coef: bfloat16 [256, 512], P('sig', 'xf'), may hold values from -6 to 6
- sym_alpha: int32 [256], P('sig'), may hold values from 0 to 1
- sym_beta: int32 [512], P('xf'), may hold values from 0 to 1
- win_target: int32 [256, 16], P('sig'), may hold values from 0 to 255
- win_pair: int32 [256, 16], P('sig'), may hold values from 0 to 31
- win_flip: int32 [256, 16], P('sig'), may hold values from 0 to 1
- rep_target: int32 [256, 512], P('sig'), may hold values from 0 to 255
- rep_pair: int32 [256, 512], P('sig'), may hold values from 0 to 4095
- rep_flip: int32 [256, 512], P('sig'), may hold values from 0 to 1
- half_ints: bfloat16 [32, 16384], P('xf'), may hold values from -0.06591797 to 0.06591797
- orbitals: bfloat16 [128, 64], replicated, may hold values from -0.5 to 0.5
- orb_sym: int32 [64], replicated, may hold values from 0 to 1
- pair_sym: int32 [32], P('xf'), may hold values from 0 to 1
Outputs:
- sigma: float32 [256, 512], P('sig', 'xf')
All inputs are finite; a program needn't handle non-finite values.
Results may differ from a plain program's by a relative error of at most 0.0041.
Values may be sent and summed in bfloat16 or wider, within the bound.
A program may use at most 64 MiB of HBM per device.

v0:
```python
import jax
import jax.numpy as jnp
from jax import lax
from jax.sharding import PartitionSpec as P


def masked_block(first, orbitals, sym_rows, sym_cols, pair_sym):
    full = jnp.einsum("pi,mpj->mij", orbitals, first, preferred_element_type=jnp.float32)
    parity = jnp.bitwise_xor(sym_rows[:, None], sym_cols[None, :])
    keep = parity[None, :, :] == pair_sym[:, None, None]
    return jnp.where(keep, full, 0.0).astype(jnp.bfloat16)


def body(
    coef,
    sym_alpha,
    sym_beta,
    win_target,
    win_pair,
    win_flip,
    rep_target,
    rep_pair,
    rep_flip,
    half_ints,
    orbitals,
    orb_sym,
    pair_sym,
):
    allowed = jnp.bitwise_xor(sym_alpha[:, None], sym_beta[None, :]) == 0
    c_eff = jnp.where(allowed, coef, jnp.zeros_like(coef))
    c_all = lax.all_gather(c_eff, "sig", axis=0, tiled=True)
    pair_rows = half_ints.shape[0]
    n_bas = orbitals.shape[0]
    n_orb = orbitals.shape[1]
    flat = half_ints.reshape(pair_rows * n_bas, n_bas)
    first = jnp.dot(flat, orbitals, preferred_element_type=jnp.float32).astype(jnp.bfloat16)
    first = first.reshape(pair_rows, n_bas, n_orb)
    local = masked_block(first, orbitals, orb_sym, orb_sym, pair_sym)
    ints = lax.all_gather(local.reshape(pair_rows, n_orb * n_orb), "xf", axis=0, tiled=True)
    columns = jnp.arange(ints.shape[0], dtype=jnp.int32)
    rows = c_all[win_target]
    picks = (
        (win_pair[:, :, None] == columns[None, None, :]) * (1 - 2 * win_flip)[:, :, None]
    ).astype(jnp.bfloat16)
    dens = jnp.einsum("aeb,aem->abm", rows, picks, preferred_element_type=jnp.float32).astype(
        jnp.bfloat16
    )
    selected = jnp.take(ints, rep_pair, axis=1)
    chosen = jnp.einsum("abm,mar->arb", dens, selected, preferred_element_type=jnp.float32)
    own_rows = rep_target.shape[0]
    n_src = own_rows * rep_target.shape[1]
    chosen = chosen.reshape(n_src, chosen.shape[2])
    flat_target = rep_target.reshape(n_src)
    flat_sign = (1 - 2 * rep_flip).astype(jnp.float32).reshape(n_src)
    targets = jnp.arange(c_all.shape[0], dtype=jnp.int32)
    signs = jnp.where(targets[:, None] == flat_target[None, :], flat_sign[None, :], 0.0)
    terms = jnp.dot(
        signs, chosen, precision=lax.Precision.HIGHEST, preferred_element_type=jnp.float32
    )
    summed = lax.psum_scatter(terms, "sig", scatter_dimension=0, tiled=True)
    return jnp.where(allowed, summed, jnp.zeros_like(summed))


def solution(mesh):
    in_specs = (
        P("sig", "xf"),
        P("sig"),
        P("xf"),
        P("sig", None),
        P("sig", None),
        P("sig", None),
        P("sig", None),
        P("sig", None),
        P("sig", None),
        P("xf", None),
        P(),
        P(),
        P("xf"),
    )
    out_specs = P("sig", "xf")
    return jax.shard_map(body, mesh=mesh, in_specs=in_specs, out_specs=out_specs, check_vma=False)
```

profile of v0, /device:TPU:0, one launch (start us, length us, event | category | flops | bytes accessed | tf_op | source)
XLA Modules:
  0.0 180.0 jit_solution(2910287823457325957)
XLA Ops:
  6.5 0.0 copy-start
  6.6 0.0 reduce-scatter.2.cloned.1.call-start
  6.6 0.8 fusion.21
  7.4 0.8 compare_and_fusion
  8.2 1.3 reshape.51
  9.5 0.8 broadcast_xor_fusion
  10.3 0.3 fusion.8
  10.6 0.9 fusion.6
  11.5 0.2 copy.21
  11.7 0.3 reshape.53
  12.0 2.1 %all_gather.6 = bf16[32,4096]{1,0:T(8,128)(2,1)S(1)} all-gather(bf16[16,4096]{1,0:T(8,128)(2,1)S(1)} %reshape.53), channel_id=1, replica_groups=mesh['sig'=16,'xf'=2] {'xf'}, dimensions={0}, use_global_device_ids=true | all-gather | bytes 393216 | tf_op jit(solution)/shard_map/all_gather | solution.py:39
  14.0 0.5 copy.22
  14.6 24.0 %gather_fusion = bf16[8192,32]{1,0:T(8,128)(2,1)S(1)} fusion(bf16[32,4096]{0,1:T(8,128)(2,1)S(1)} %copy.22, s32[8192]{0:T(1024)S(1)} %broadcast_clamp_fusion), kind=kCustom, calls=%fused_computation | custom fusion | bytes 1081344 | tf_op jit(solution)/shard_map/jit(_take)/gather | solution.py:48
  38.6 0.8 copy.23
  39.4 0.1 fusion.24
  39.5 43.0 %all_gather.7 = bf16[256,256]{1,0:T(8,128)(2,1)S(1)} all-gather(bf16[16,256]{1,0:T(8,128)(2,1)S(1)} %fusion.24), channel_id=1, replica_groups=mesh['sig'=16,'xf'=2] {'sig'}, dimensions={0}, use_global_device_ids=true | all-gather | bytes 139264 | tf_op jit(solution)/shard_map/all_gather | solution.py:31
  82.5 0.1 reshape.65
  82.7 1.2 gather_fusion.1
  83.8 0.0 copy-done.3
  83.8 4.8 %fusion.7 = f32[16,512,256]{2,1,0:T(8,128)} fusion(bf16[16,16,256]{2,1,0:T(8,128)(2,1)S(1)} %bitcast.34, bf16[16,512,32]{1,2,0:T(8,128)(2,1)S(1)} %copy.23, pred[16,512]{1,0:T(8,128)(4,1)S(1)} %compare_and_fusion, s32[16,16]{1,0:T(8,128)S(1)} %multiply_subtract_fusion, s32[16,16]{1,0:T(8,128)S(1)} %copy-done.3), kind=kOutput, calls=%fused_computation.13 | convolution fusion | flops 138829824 | bytes 9054208 | tf_op jit(solution)/shard_map/abm,mar->arb/dot_general | solution.py:49
  88.6 11.0 %fusion = f32[256,256]{1,0:T(8,128)} fusion(f32[8192,256]{1,0:T(8,128)} %bitcast.32, f32[8192]{0:T(1024)S(1)} %bitcast.37, s32[8192]{0:T(1024)S(1)} %bitcast.38), kind=kOutput, calls=%fused_computation.2 | convolution fusion | flops 6446645248 | bytes 8716288 | tf_op jit(solution)/shard_map/dot_general | solution.py:57
  99.6 0.0 reduce-scatter.2.cloned.1.call-update
  99.6 72.2 %reduce-scatter.2.cloned.1.call-done = f32[16,256]{1,0:T(8,128)} async-done(((f32[256,256]{1,0:T(8,128)}), f32[16,256]{1,0:T(8,128)}) %reduce-scatter.2.cloned.1.call-update) | async-done | bytes 16400 | tf_op jit(solution)/shard_map/reduce_scatter | solution.py:60
  171.8 1.4 fusion.23
  (24 shorter events, 0.1 us)
Async XLA Ops:
  6.5 3.8 %copy-start = (bf16[128,64]{0,1:T(8,128)(2,1)S(1)}, bf16[128,64]{0,1:T(8,128)(2,1)}, u32[]{:S(2)}) copy-start(bf16[128,64]{0,1:T(8,128)(2,1)} %param.23) | copy-start | bytes 49156
  6.5 32.9 %copy-start.4 = (bf16[16,256]{1,0:T(8,128)(2,1)S(1)}, bf16[16,256]{1,0:T(8,128)(2,1)}, u32[]{:S(2)}) copy-start(bf16[16,256]{1,0:T(8,128)(2,1)} %param.13) | copy-start | bytes 24580
  6.5 32.9 %copy-start.8 = (s32[16]{0:T(128)S(1)}, s32[16]{0:T(128)}, u32[]{:S(2)}) copy-start(s32[16]{0:T(128)} %param.14) | copy-start | bytes 196
  6.5 32.9 %copy-start.7 = (s32[256]{0:T(256)S(1)}, s32[256]{0:T(256)}, u32[]{:S(2)}) copy-start(s32[256]{0:T(256)} %param.15) | copy-start | bytes 3076
  6.5 75.9 %copy-start.5 = (s32[16,16]{1,0:T(8,128)S(1)}, s32[16,16]{1,0:T(8,128)}, u32[]{:S(2)}) copy-start(s32[16,16]{1,0:T(8,128)} %param.16) | copy-start | bytes 3076
  6.5 76.0 %copy-start.6 = (s32[16,16]{1,0:T(8,128)S(1)}, s32[16,16]{1,0:T(8,128)}, u32[]{:S(2)}) copy-start(s32[16,16]{1,0:T(8,128)} %param.18) | copy-start | bytes 3076
  6.6 76.0 %copy-start.1 = (s32[16,512]{1,0:T(8,128)S(1)}, s32[16,512]{1,0:T(8,128)}, u32[]{:S(2)}) copy-start(s32[16,512]{1,0:T(8,128)} %param.21) | copy-start | bytes 98308
  6.6 76.1 %copy-start.2 = (s32[16,512]{1,0:T(8,128)S(1)}, s32[16,512]{1,0:T(8,128)}, u32[]{:S(2)}) copy-start(s32[16,512]{1,0:T(8,128)} %param.19) | copy-start | bytes 98308
  6.6 77.2 %copy-start.3 = (s32[16,16]{1,0:T(8,128)S(1)}, s32[16,16]{1,0:T(8,128)}, u32[]{:S(2)}) copy-start(s32[16,16]{1,0:T(8,128)} %param.17) | copy-start | bytes 3076
  6.6 165.2 %reduce-scatter.2.cloned.1.call-start = ((), (), s32[]{:S(2)}) async-start(), calls=%async_computation.1 | async-start | bytes 278528 | tf_op jit(solution)/shard_map/reduce_scatter | solution.py:60
Sparse Core Ops, SparseCore 0:
  99.7 72.0 reduce-scatter.1
where the time goes:
time: 180 us
  waiting for transfers between devices  72.2 us (40%)
  blocking collectives  45 us (25%)
  local copies, waits for them, and re-layouts  28.3 us (16%)
  matrix products  16.9 us (9%)
  between operations  13.6 us (8%)
  other arithmetic  3.88 us (2%)
    reduce_scatter x1, waiting for transfers between devices, body(): summed = lax.psum_scatter(terms, 'sig', scatter_dimension=0, tiled=True)  72.2 us
    all_gather x1, blocking collectives, body(): c_all = lax.all_gather(c_eff, 'sig', axis=0, tiled=True)  43 us
    gather x2, local copies, waits for them, and re-layouts, body(): selected = jnp.take(ints, rep_pair, axis=1)  24.8 us
    dot_general x1, matrix products, body(): jnp.dot(signs, chosen, precision=lax.Precision.HIGHEST, preferred_element...  11 us
    dot_general x1, matrix products, body(): jnp.einsum('abm,mar->arb', dens, selected, preferred_element_type=jnp.flo...  4.78 us
  transfers between devices with their start and end apart: 1, of which 1 were waited for; matrix products, arithmetic and copies ran while one was open for 0% of the time, Pallas kernels for 0%

commit v1 on v0

v1 whole, which is shorter than its diff:
```python
import functools

import jax
import jax.numpy as jnp
from jax import lax
from jax.experimental import pallas as pl
from jax.experimental.pallas import tpu as pltpu
from jax.sharding import PartitionSpec as P

MESH = pl.DeviceIdType.MESH
NT = (((1,), (1,)), ((), ()))
TN = (((0,), (0,)), ((), ()))
NN = (((1,), (0,)), ((), ()))
F32 = jnp.float32
BF16 = jnp.bfloat16
LANES = 128


def dot(x, y, dims):
    return lax.dot_general(x, y, dims, preferred_element_type=F32)


def split(x):
    high = x.astype(BF16)
    return high, (x - high.astype(F32)).astype(BF16)


def for_each(count, step):
    if count <= 2:
        for index in range(count):
            step(index)
    else:
        lax.fori_loop(0, count, lambda index, _: (step(index), 0)[1], 0)


def column(row, count):
    n = row.shape[1]
    mine = lax.broadcasted_iota(jnp.int32, (count, n), 0)
    other = lax.broadcasted_iota(jnp.int32, (count, n), 1)
    return jnp.sum(jnp.where(mine == other, row, 0), axis=1, keepdims=True)


def transform(half_ref, orb_ref, orb_sym_ref, pair_sym_ref, first_ref, block_ref, table_ref):
    rows = half_ref.shape[0]
    n_bas, n_orb = orb_ref.shape
    half = n_orb * n_orb // LANES
    orb = orb_ref[...]
    twice = jnp.concatenate([orb, orb], axis=1)
    group = 16

    def first_step(c):
        base = c * group * n_bas
        parts = [half_ref[:, pl.ds(pl.multiple_of(base + k * n_bas, LANES), n_bas)] for k in range(group)]
        first = dot(jnp.concatenate(parts, axis=0), twice, NN)
        start = pl.multiple_of(c * (group * rows), group * rows)
        first_ref[pl.ds(start, group * rows), :] = first.astype(BF16).astype(F32)

    for c in range(n_bas // group):
        first_step(c)

    lane = lax.broadcasted_iota(jnp.int32, (half, LANES), 1)
    low = lane < n_orb
    sym = orb_sym_ref[...].reshape(1, n_orb)
    sym_i = column(sym, n_orb)
    parity = jnp.bitwise_xor(
        jnp.where(low, sym_i[:half], sym_i[half:]), jnp.concatenate([sym, sym], axis=1)
    )
    orb_t = orb.astype(F32).T.astype(BF16)
    for m in range(rows):
        part = first_ref[pl.ds(m, n_bas, stride=rows), :].astype(BF16)
        full = dot(orb_t, part, NN)
        full = jnp.where(low, full[:half], full[half:])
        full = jnp.where(parity == pair_sym_ref[m], full, 0.0)
        block_ref[m * half : (m + 1) * half, :] = full.astype(BF16).astype(F32)
    for h in range(half):
        table_ref[h * rows : (h + 1) * rows, :] = block_ref[pl.ds(h, rows, stride=half), :]


def couple(a, own, n_orb, win, rep, table_ref, g_ref, w_ref):
    win_target_ref, win_pair_ref, win_flip_ref = win
    rep_target_ref, rep_pair_ref, rep_flip_ref = rep
    half = n_orb * n_orb // LANES
    rows = table_ref.shape[0] // half
    n_all = g_ref.shape[1]
    n_rep = rep_pair_ref.shape[1]
    row = pl.ds(a, 1)
    pair = rep_pair_ref[row, :]
    orb_i = pair // n_orb
    orb_j = pair % n_orb
    place = (orb_i // half) * n_orb + orb_j
    which = orb_i % half
    blocks = n_rep // LANES
    places = [jnp.broadcast_to(place[:, k * LANES : (k + 1) * LANES], (8, LANES)) for k in range(blocks)]
    whiches = [jnp.broadcast_to(which[:, k * LANES : (k + 1) * LANES], (8, LANES)) for k in range(blocks)]
    picked = [[jnp.zeros((8, LANES), F32) for _ in range(rows // 8)] for _ in range(blocks)]
    for h in range(half):
        hits = [whiches[k] == h for k in range(blocks)]
        for s in range(rows // 8):
            table = table_ref[h * rows + s * 8 : h * rows + (s + 1) * 8, :]
            for k in range(blocks):
                got = jnp.take_along_axis(table, places[k], axis=1, mode="promise_in_bounds")
                picked[k][s] = jnp.where(hits[k], got, picked[k][s])
    chosen = jnp.concatenate([jnp.concatenate(p, axis=0) for p in picked], axis=1)
    sign = (1 - 2 * rep_flip_ref[row, :]).astype(F32)
    chosen = (chosen * sign).astype(BF16)
    target = rep_target_ref[row, :]
    w_target = win_target_ref[row, :]
    w_pair = win_pair_ref[row, :]
    w_sign = (1 - 2 * win_flip_ref[row, :]).astype(F32)
    n_win = w_pair.shape[1]
    m_own = lax.broadcasted_iota(jnp.int32, (rows, n_win), 0) + own * rows
    picks = jnp.where(m_own == w_pair, w_sign, 0.0).astype(BF16)
    store = pl.ds(pl.multiple_of(a * rows, rows), rows)
    tile = 256

    def strings(k):
        base = k * tile
        t = lax.broadcasted_iota(jnp.int32, (tile, n_rep), 0) + base
        hit = jnp.where(t == target, 1.0, 0.0).astype(BF16)
        s = lax.broadcasted_iota(jnp.int32, (tile, n_win), 0) + base
        reach = jnp.where(s == w_target, 1.0, 0.0).astype(BF16)
        cols = pl.ds(pl.multiple_of(base, tile), tile)
        g_ref[store, cols] = dot(chosen, hit, NT)
        w_ref[store, cols] = dot(picks, reach, NT)

    for_each(n_all // tile, strings)


def kernel(
    n_sig, n_xf,
    coef_ref, sym_alpha_ref, sym_beta_ref,
    win_target_ref, win_pair_ref, win_flip_ref,
    rep_target_ref, rep_pair_ref, rep_flip_ref,
    half_ref, orb_ref, orb_sym_ref, pair_sym_ref,
    out_ref,
    first_ref, block_ref, table_ref, g_ref, w_ref,
    c_ref, q_ref, q_in, p_ref, p_in, h_ref,
    c_send, c_recv, q_send, q_recv, p_send, p_recv, h_send, h_recv,
):
    me = lax.axis_index("sig")
    own = lax.axis_index("xf")
    own_rows, n_beta = coef_ref.shape
    n_orb = orb_ref.shape[1]
    n_all = own_rows * n_sig
    width = n_all // n_xf

    barrier = pltpu.get_barrier_semaphore()

    def greet_sig(k):
        pl.semaphore_signal(barrier, inc=1, device_id=(lax.rem(me + k, n_sig), own), device_id_type=MESH)

    def greet_xf(k):
        pl.semaphore_signal(barrier, inc=1, device_id=(me, lax.rem(own + k, n_xf)), device_id_type=MESH)

    for k in range(1, n_sig):
        greet_sig(k)
    for k in range(1, n_xf):
        greet_xf(k)

    sym_alpha = column(sym_alpha_ref[...].reshape(1, own_rows), own_rows)
    sym_beta = sym_beta_ref[...].reshape(1, n_beta)
    allowed = jnp.bitwise_xor(sym_alpha, sym_beta) == 0
    c_ref[me] = jnp.where(allowed, coef_ref[...].astype(F32), 0.0).astype(BF16)

    transform(half_ref, orb_ref, orb_sym_ref, pair_sym_ref, first_ref, block_ref, table_ref)

    pl.semaphore_wait(barrier, n_sig + n_xf - 2)

    def c_copy(k):
        return pltpu.make_async_remote_copy(
            src_ref=c_ref.at[me], dst_ref=c_ref.at[me], send_sem=c_send.at[k], recv_sem=c_recv.at[k],
            device_id=(lax.rem(me + k, n_sig), own), device_id_type=MESH)

    def c_arrival(k):
        slot = lax.rem(me + n_sig - k, n_sig)
        return pltpu.make_async_remote_copy(
            src_ref=c_ref.at[slot], dst_ref=c_ref.at[slot], send_sem=c_send.at[k], recv_sem=c_recv.at[k],
            device_id=(lax.rem(me + k, n_sig), own), device_id_type=MESH)

    def loop(low, high, step):
        lax.fori_loop(low, high, lambda k, _: (step(k), 0)[1], 0)

    loop(1, n_sig, lambda k: c_copy(k).start())

    win = (win_target_ref, win_pair_ref, win_flip_ref)
    rep = (rep_target_ref, rep_pair_ref, rep_flip_ref)
    loop(0, own_rows, lambda a: couple(a, own, n_orb, win, rep, table_ref, g_ref, w_ref))

    depth = g_ref.shape[0]
    tile = 256

    def q_tile(t, x):
        cols = pl.ds(pl.multiple_of(t * tile, tile), tile)
        lanes = pl.ds(pl.multiple_of(x * width, width), width)
        if depth == tile:
            high, low = split(g_ref[:, cols])
            w = w_ref[:, lanes].astype(BF16)
            total = dot(high, w, TN) + dot(low, w, TN)
        else:
            def part(k, total):
                ks = pl.ds(pl.multiple_of(k * tile, tile), tile)
                high, low = split(g_ref[ks, cols])
                w = w_ref[ks, lanes].astype(BF16)
                return total + dot(high, w, TN) + dot(low, w, TN)
            total = lax.fori_loop(0, depth // tile, part, jnp.zeros((tile, width), F32))
        q_ref[x, cols, :] = total

    for_each(n_xf, lambda x: for_each(n_all // tile, lambda t: q_tile(t, x)))

    def q_copy(k):
        there = lax.rem(own + k, n_xf)
        return pltpu.make_async_remote_copy(
            src_ref=q_ref.at[there], dst_ref=q_in.at[k - 1], send_sem=q_send.at[k - 1], recv_sem=q_recv.at[k - 1],
            device_id=(me, there), device_id_type=MESH)

    for k in range(1, n_xf):
        q_copy(k).start()
    for k in range(1, n_xf):
        q_copy(k).wait_recv()

    def p_block(t):
        rows = pl.ds(pl.multiple_of(t * tile, tile), tile)
        total = q_ref[own, rows, :]
        for k in range(n_xf - 1):
            total = total + q_in[k, rows, :]
        per = tile // own_rows
        p_ref[pl.ds(t * per, per)] = total.astype(BF16).reshape(per, own_rows, width)

    for_each(n_all // tile, p_block)

    def p_copy(k):
        there = lax.rem(me + k, n_sig)
        return pltpu.make_async_remote_copy(
            src_ref=p_ref.at[there], dst_ref=p_in.at[k], send_sem=p_send.at[k], recv_sem=p_recv.at[k],
            device_id=(there, own), device_id_type=MESH)

    loop(1, n_sig, lambda k: p_copy(k).start())
    p_in[0] = p_ref[me]
    loop(1, n_sig, lambda k: p_copy(k).wait_recv())
    h_ref[own] = jnp.sum(p_in[...].astype(F32), axis=0)

    def h_copy(k):
        return pltpu.make_async_remote_copy(
            src_ref=h_ref.at[own], dst_ref=h_ref.at[own], send_sem=h_send.at[k - 1], recv_sem=h_recv.at[k - 1],
            device_id=(me, lax.rem(own + k, n_xf)), device_id_type=MESH)

    def h_arrival(k):
        slot = lax.rem(own + n_xf - k, n_xf)
        return pltpu.make_async_remote_copy(
            src_ref=h_ref.at[slot], dst_ref=h_ref.at[slot], send_sem=h_send.at[k - 1], recv_sem=h_recv.at[k - 1],
            device_id=(me, lax.rem(own + k, n_xf)), device_id_type=MESH)

    for k in range(1, n_xf):
        h_copy(k).start()
    loop(1, n_sig, lambda k: c_arrival(k).wait_recv())
    for k in range(1, n_xf):
        h_arrival(k).wait_recv()
    high, low = split(jnp.concatenate([h_ref[x] for x in range(n_xf)], axis=1))
    c_all = c_ref[...].reshape(n_all, n_beta)
    total = dot(high, c_all, NN) + dot(low, c_all, NN)
    out_ref[...] = jnp.where(allowed, total, 0.0)

    loop(1, n_sig, lambda k: c_copy(k).wait_send())
    loop(1, n_sig, lambda k: p_copy(k).wait_send())
    for k in range(1, n_xf):
        q_copy(k).wait_send()
        h_copy(k).wait_send()


def body(n_sig, n_xf, *args):
    coef, half_ints, orbitals = args[0], args[9], args[10]
    own_rows, n_beta = coef.shape
    rows = half_ints.shape[0]
    n_bas, n_orb = orbitals.shape
    n_all = own_rows * n_sig
    width = n_all // n_xf
    half = n_orb * n_orb // LANES
    vmem = pl.BlockSpec(memory_space=pltpu.VMEM)
    smem = pl.BlockSpec(memory_space=pltpu.SMEM)
    dma = pltpu.SemaphoreType.DMA
    return pl.pallas_call(
        functools.partial(kernel, n_sig, n_xf),
        out_shape=jax.ShapeDtypeStruct((own_rows, n_beta), F32),
        in_specs=[vmem] * 12 + [smem],
        out_specs=vmem,
        scratch_shapes=[
            pltpu.VMEM((n_bas * rows, LANES), F32),
            pltpu.VMEM((rows * half, LANES), F32),
            pltpu.VMEM((rows * half, LANES), F32),
            pltpu.VMEM((own_rows * rows, n_all), F32),
            pltpu.VMEM((own_rows * rows, n_all), F32),
            pltpu.VMEM((n_sig, own_rows, n_beta), BF16),
            pltpu.VMEM((n_xf, n_all, width), F32),
            pltpu.VMEM((n_xf - 1, n_all, width), F32),
            pltpu.VMEM((n_sig, own_rows, width), BF16),
            pltpu.VMEM((n_sig, own_rows, width), BF16),
            pltpu.VMEM((n_xf, own_rows, width), F32),
            dma((n_sig,)), dma((n_sig,)),
            dma((n_xf - 1,)), dma((n_xf - 1,)),
            dma((n_sig,)), dma((n_sig,)),
            dma((n_xf - 1,)), dma((n_xf - 1,)),
        ],
        compiler_params=pltpu.CompilerParams(
            collective_id=0, has_side_effects=True, vmem_limit_bytes=40 * 1024 * 1024
        ),
    )(*args)


def solution(mesh):
    in_specs = (
        P("sig", "xf"), P("sig"), P("xf"),
        P("sig", None), P("sig", None), P("sig", None),
        P("sig", None), P("sig", None), P("sig", None),
        P("xf", None), P(), P(), P("xf"),
    )
    step = functools.partial(body, mesh.shape["sig"], mesh.shape["xf"])
    return jax.shard_map(step, mesh=mesh, in_specs=in_specs, out_specs=P("sig", "xf"), check_vma=False)
```

time: 180 us -> 35.7 us (0.20)
  waiting for transfers between devices: 72.2 us -> 0 us
  blocking collectives: 45 us -> 0 us
  Pallas kernels: 0 us -> 27.1 us
  local copies, waits for them, and re-layouts: 28.3 us -> 8.04 us
  matrix products: 16.9 us -> 0 us
  between operations: 13.6 us -> 0.05 us
  other arithmetic: 3.88 us -> 0 us
    reduce_scatter x1 -> x0, waiting for transfers between devices: 72.2 us -> none  [body(): summed = lax.psum_scatter(terms, 'sig', scatter_dimension=0, tiled=True)]
    all_gather x2 -> x0, blocking collectives: 45 us -> none  [the longest x1 43 us: body(): c_all = lax.all_gather(c_eff, 'sig', axis=0, tiled=True)]
    pallas_call x0 -> x1, Pallas kernels: none -> 27.1 us  [body(): pl.pallas_call(functools.partial(kernel, n_sig, n_xf), out_shape=jax.Shap...]
    gather x3 -> x0, local copies, waits for them, and re-layouts: 26 us -> none  [the longest x2 24.8 us: body(): selected = jnp.take(ints, rep_pair, axis=1)]
    dot_general x4 -> x0, matrix products: 16.9 us -> none  [the longest x1 11 us: body(): jnp.dot(signs, chosen, precision=lax.Precision.HIGHEST, preferred_element...]
    unnamed x21 -> x26, local copies, waits for them, and re-layouts: 0.07 us -> 8.04 us
  transfers between devices with their start and end apart: 1 -> 0, of which waited for: 1 -> 0; matrix products, arithmetic and copies ran while one was open for 0% -> 0% of each run, Pallas kernels for 0% -> 0%
where the time goes in v1:
time: 35.7 us; the launch traced here: 35.2 us
  Pallas kernels  27.1 us (76%)
  local copies, waits for them, and re-layouts  8.04 us (23%)
    pallas_call x1, Pallas kernels, body(): pl.pallas_call(functools.partial(kernel, n_sig, n_xf), out_shape=jax.Shap...  27.1 us
    unnamed x26, local copies, waits for them, and re-layouts  8.04 us

profile of v1, /device:TPU:0, one launch (start us, length us, event | category | flops | bytes accessed | tf_op | source)
XLA Modules:
  0.0 35.2 jit_solution(3906550692163497389)
XLA Ops:
  0.0 0.0 copy-start.1
  0.0 0.0 copy-start.5
  0.0 0.8 %copy.14.orb_ref = bf16[128,64]{1,0:T(8,128)(2,1)S(1)} copy(bf16[128,64]{0,1:T(8,128)(2,1)} %param.23) | data formatting | bytes 32768 | tf_op args[10]
  0.8 0.0 copy-done.1
  0.9 0.0 copy-done.5
  0.9 0.0 copy-done.4
  0.9 0.0 copy-start
  0.9 1.0 %copy-done = bf16[16,16384]{1,0:T(8,128)(2,1)S(1)} copy-done((bf16[16,16384]{1,0:T(8,128)(2,1)S(1)}, bf16[16,16384]{1,0:T(8,128)(2,1)}, u32[]{:S(2)}) %copy-start) | copy-done | bytes 524312
  1.9 0.0 copy-start.2
  1.9 0.8 %copy-done.2 = s32[16,512]{1,0:T(8,128)S(1)} copy-done((s32[16,512]{1,0:T(8,128)S(1)}, s32[16,512]{1,0:T(8,128)}, u32[]{:S(2)}) %copy-start.2) | copy-done | bytes 32792
  2.7 0.0 copy-start.3
  2.7 0.8 %copy-done.3 = s32[16,512]{1,0:T(8,128)S(1)} copy-done((s32[16,512]{1,0:T(8,128)S(1)}, s32[16,512]{1,0:T(8,128)}, u32[]{:S(2)}) %copy-start.3) | copy-done | bytes 32792
  3.4 0.0 copy-start.6
  3.4 0.7 %copy-done.6 = s32[16,16]{1,0:T(8,128)S(1)} copy-done((s32[16,16]{1,0:T(8,128)S(1)}, s32[16,16]{1,0:T(8,128)}, u32[]{:S(2)}) %copy-start.6) | copy-done | bytes 1048
  4.1 0.0 copy-start.7
  4.1 0.7 %copy-done.7 = s32[16,16]{1,0:T(8,128)S(1)} copy-done((s32[16,16]{1,0:T(8,128)S(1)}, s32[16,16]{1,0:T(8,128)}, u32[]{:S(2)}) %copy-start.7) | copy-done | bytes 1048
  4.8 0.0 copy-start.8
  4.8 0.7 %copy-done.8 = s32[256]{0:T(256)S(1)} copy-done((s32[256]{0:T(256)S(1)}, s32[256]{0:T(256)}, u32[]{:S(2)}) %copy-start.8) | copy-done | bytes 1048
  5.5 0.0 copy-start.9
  5.5 0.7 %copy-done.9 = s32[16]{0:T(128)S(1)} copy-done((s32[16]{0:T(128)S(1)}, s32[16]{0:T(128)}, u32[]{:S(2)}) %copy-start.9) | copy-done | bytes 88
  6.2 0.7 %copy-done.10 = s32[64]{0:T(128)S(1)} copy-done((s32[64]{0:T(128)S(1)}, s32[64]{0:T(128)}, u32[]{:S(2)}) %copy-start.10) | copy-done | bytes 280
  6.8 0.7 %copy-done.11 = s32[16]{0:T(128)S(1)} copy-done((s32[16]{0:T(128)S(1)}, s32[16]{0:T(128)}, u32[]{:S(2)}) %copy-start.11) | copy-done | bytes 88
  7.5 27.1 %shard_map.127 = f32[16,256]{1,0:T(8,128)S(1)} custom-call(bf16[16,256]{1,0:T(8,128)(2,1)S(1)} %copy-done.4, s32[16]{0:T(128)S(1)} %copy-done.9, s32[256]{0:T(256)S(1)} %copy-done.8, s32[16,16]{1,0:T(8,128)S(1)} %copy-done.5, s32[16,16]{1,0:T(8,128)S(1)} %copy-done.6, s32[16,16]{1,0:T(8,128)S(1)} %copy-done.7, s32[16,512]{1,0:T(8,128)S(1)} %copy-done.1, ...), custom_call_target="tpu_custom_call" | custom-call | tf_op jit(solution)/shard_map/pallas_call | solution.py:281
  34.6 0.6 %copy.16 = f32[16,256]{1,0:T(8,128)} copy(f32[16,256]{1,0:T(8,128)S(1)} %shard_map.127) | data formatting | bytes 32768
  (3 shorter events, 0.0 us)
Async XLA Ops:
  0.0 0.8 %copy-start.1 = (s32[16,512]{1,0:T(8,128)S(1)}, s32[16,512]{1,0:T(8,128)}, u32[]{:S(2)}) copy-start(s32[16,512]{1,0:T(8,128)} %rep_target_ref.1) | copy-start | bytes 98308
  0.0 0.8 %copy-start.5 = (s32[16,16]{1,0:T(8,128)S(1)}, s32[16,16]{1,0:T(8,128)}, u32[]{:S(2)}) copy-start(s32[16,16]{1,0:T(8,128)} %win_target_ref.1) | copy-start | bytes 3076
  0.0 0.9 %copy-start.4 = (bf16[16,256]{1,0:T(8,128)(2,1)S(1)}, bf16[16,256]{1,0:T(8,128)(2,1)}, u32[]{:S(2)}) copy-start(bf16[16,256]{1,0:T(8,128)(2,1)} %coef_ref.1) | copy-start | bytes 24580
  0.9 1.0 %copy-start = (bf16[16,16384]{1,0:T(8,128)(2,1)S(1)}, bf16[16,16384]{1,0:T(8,128)(2,1)}, u32[]{:S(2)}) copy-start(bf16[16,16384]{1,0:T(8,128)(2,1)} %half_ref.1) | copy-start | bytes 1572868
  1.9 0.8 %copy-start.2 = (s32[16,512]{1,0:T(8,128)S(1)}, s32[16,512]{1,0:T(8,128)}, u32[]{:S(2)}) copy-start(s32[16,512]{1,0:T(8,128)} %rep_pair_ref.1) | copy-start | bytes 98308
  2.7 0.8 %copy-start.3 = (s32[16,512]{1,0:T(8,128)S(1)}, s32[16,512]{1,0:T(8,128)}, u32[]{:S(2)}) copy-start(s32[16,512]{1,0:T(8,128)} %rep_flip_ref.1) | copy-start | bytes 98308
  3.4 0.7 %copy-start.6 = (s32[16,16]{1,0:T(8,128)S(1)}, s32[16,16]{1,0:T(8,128)}, u32[]{:S(2)}) copy-start(s32[16,16]{1,0:T(8,128)} %win_pair_ref.1) | copy-start | bytes 3076
  4.1 0.7 %copy-start.7 = (s32[16,16]{1,0:T(8,128)S(1)}, s32[16,16]{1,0:T(8,128)}, u32[]{:S(2)}) copy-start(s32[16,16]{1,0:T(8,128)} %win_flip_ref.1) | copy-start | bytes 3076
  4.8 0.7 %copy-start.8 = (s32[256]{0:T(256)S(1)}, s32[256]{0:T(256)}, u32[]{:S(2)}) copy-start(s32[256]{0:T(256)} %sym_beta_ref.1) | copy-start | bytes 3076
  5.5 0.7 %copy-start.9 = (s32[16]{0:T(128)S(1)}, s32[16]{0:T(128)}, u32[]{:S(2)}) copy-start(s32[16]{0:T(128)} %sym_alpha_ref.1) | copy-start | bytes 196
  6.2 0.7 %copy-start.10 = (s32[64]{0:T(128)S(1)}, s32[64]{0:T(128)}, u32[]{:S(2)}) copy-start(s32[64]{0:T(128)} %orb_sym_ref.1) | copy-start | bytes 772
  6.8 0.7 %copy-start.11 = (s32[16]{0:T(128)S(1)}, s32[16]{0:T(128)}, u32[]{:S(2)}) copy-start(s32[16]{0:T(128)} %pair_sym_ref.1) | copy-start | bytes 196

commit v2 on v1

--- a/solution.py
+++ b/solution.py
@@ -14,6 +14,7 @@
 F32 = jnp.float32
 BF16 = jnp.bfloat16
 LANES = 128
+WIDE = 256
 
 
 def dot(x, y, dims):
@@ -42,108 +43,108 @@
 
 def transform(half_ref, orb_ref, orb_sym_ref, pair_sym_ref, first_ref, block_ref, table_ref):
     rows = half_ref.shape[0]
-    n_bas, n_orb = orb_ref.shape
-    half = n_orb * n_orb // LANES
-    orb = orb_ref[...]
-    twice = jnp.concatenate([orb, orb], axis=1)
+    n_orb, n_bas = orb_ref.shape
+    orb_t = orb_ref[...]
+    twice = jnp.concatenate([orb_t, orb_t], axis=0)
     group = 16
 
-    def first_step(c):
+    for c in range(n_bas // group):
         base = c * group * n_bas
-        parts = [half_ref[:, pl.ds(pl.multiple_of(base + k * n_bas, LANES), n_bas)] for k in range(group)]
-        first = dot(jnp.concatenate(parts, axis=0), twice, NN)
-        start = pl.multiple_of(c * (group * rows), group * rows)
-        first_ref[pl.ds(start, group * rows), :] = first.astype(BF16).astype(F32)
-
-    for c in range(n_bas // group):
-        first_step(c)
-
-    lane = lax.broadcasted_iota(jnp.int32, (half, LANES), 1)
-    low = lane < n_orb
+        parts = [half_ref[:, base + k * n_bas : base + (k + 1) * n_bas] for k in range(group)]
+        first = dot(jnp.concatenate(parts, axis=0), twice, NT)
+        start = c * (group * rows)
+        first_ref[start : start + group * rows, :] = first.astype(BF16).astype(F32)
+
     sym = orb_sym_ref[...].reshape(1, n_orb)
-    sym_i = column(sym, n_orb)
-    parity = jnp.bitwise_xor(
-        jnp.where(low, sym_i[:half], sym_i[half:]), jnp.concatenate([sym, sym], axis=1)
-    )
-    orb_t = orb.astype(F32).T.astype(BF16)
+    parity = jnp.bitwise_xor(column(sym, n_orb), jnp.concatenate([sym, sym], axis=1))
     for m in range(rows):
         part = first_ref[pl.ds(m, n_bas, stride=rows), :].astype(BF16)
         full = dot(orb_t, part, NN)
-        full = jnp.where(low, full[:half], full[half:])
-        full = jnp.where(parity == pair_sym_ref[m], full, 0.0)
-        block_ref[m * half : (m + 1) * half, :] = full.astype(BF16).astype(F32)
-    for h in range(half):
-        table_ref[h * rows : (h + 1) * rows, :] = block_ref[pl.ds(h, rows, stride=half), :]
-
-
-def couple(a, own, n_orb, win, rep, table_ref, g_ref, w_ref):
+        block_ref[m * n_orb : (m + 1) * n_orb, :] = jnp.where(parity == pair_sym_ref[m], full, 0.0)
+    low = lax.broadcasted_iota(jnp.int32, (rows, LANES), 1) < n_orb
+    for h in range(n_orb * n_orb // WIDE):
+        each = [block_ref[pl.ds(h * 4 + i, rows, stride=n_orb), :] for i in range(4)]
+        left = jnp.where(low, each[0], each[1])
+        right = jnp.where(low, each[2], each[3])
+        table_ref[h * rows : (h + 1) * rows, :] = jnp.concatenate([left, right], axis=1).astype(BF16)
+
+
+def couple(strings, own, win, rep, table_ref, g_ref, w_ref):
     win_target_ref, win_pair_ref, win_flip_ref = win
     rep_target_ref, rep_pair_ref, rep_flip_ref = rep
-    half = n_orb * n_orb // LANES
-    rows = table_ref.shape[0] // half
+    groups = table_ref.shape[0] // 16
+    rows = 16
     n_all = g_ref.shape[1]
     n_rep = rep_pair_ref.shape[1]
-    row = pl.ds(a, 1)
-    pair = rep_pair_ref[row, :]
-    orb_i = pair // n_orb
-    orb_j = pair % n_orb
-    place = (orb_i // half) * n_orb + orb_j
-    which = orb_i % half
-    blocks = n_rep // LANES
-    places = [jnp.broadcast_to(place[:, k * LANES : (k + 1) * LANES], (8, LANES)) for k in range(blocks)]
-    whiches = [jnp.broadcast_to(which[:, k * LANES : (k + 1) * LANES], (8, LANES)) for k in range(blocks)]
-    picked = [[jnp.zeros((8, LANES), F32) for _ in range(rows // 8)] for _ in range(blocks)]
-    for h in range(half):
-        hits = [whiches[k] == h for k in range(blocks)]
-        for s in range(rows // 8):
-            table = table_ref[h * rows + s * 8 : h * rows + (s + 1) * 8, :]
-            for k in range(blocks):
-                got = jnp.take_along_axis(table, places[k], axis=1, mode="promise_in_bounds")
-                picked[k][s] = jnp.where(hits[k], got, picked[k][s])
-    chosen = jnp.concatenate([jnp.concatenate(p, axis=0) for p in picked], axis=1)
-    sign = (1 - 2 * rep_flip_ref[row, :]).astype(F32)
-    chosen = (chosen * sign).astype(BF16)
-    target = rep_target_ref[row, :]
-    w_target = win_target_ref[row, :]
-    w_pair = win_pair_ref[row, :]
-    w_sign = (1 - 2 * win_flip_ref[row, :]).astype(F32)
-    n_win = w_pair.shape[1]
+    n_win = win_pair_ref.shape[1]
+    table = table_ref[...]
+    inner = lax.broadcasted_iota(jnp.int32, (WIDE, n_rep), 0)
     m_own = lax.broadcasted_iota(jnp.int32, (rows, n_win), 0) + own * rows
-    picks = jnp.where(m_own == w_pair, w_sign, 0.0).astype(BF16)
-    store = pl.ds(pl.multiple_of(a * rows, rows), rows)
-    tile = 256
-
-    def strings(k):
-        base = k * tile
-        t = lax.broadcasted_iota(jnp.int32, (tile, n_rep), 0) + base
-        hit = jnp.where(t == target, 1.0, 0.0).astype(BF16)
-        s = lax.broadcasted_iota(jnp.int32, (tile, n_win), 0) + base
-        reach = jnp.where(s == w_target, 1.0, 0.0).astype(BF16)
-        cols = pl.ds(pl.multiple_of(base, tile), tile)
-        g_ref[store, cols] = dot(chosen, hit, NT)
-        w_ref[store, cols] = dot(picks, reach, NT)
-
-    for_each(n_all // tile, strings)
+    wide = []
+    for a in strings:
+        pair = rep_pair_ref[pl.ds(a, 1), :]
+        spot = jnp.bitwise_and(pair, WIDE - 1)
+        hit = jnp.where(inner == spot, 1.0, 0.0).astype(BF16)
+        wide.append(dot(table, hit, NN))
+    chosen, picks = [], []
+    for a, y in zip(strings, wide):
+        row = pl.ds(a, 1)
+        group = jnp.broadcast_to(jnp.right_shift(rep_pair_ref[row, :], WIDE.bit_length() - 1), (rows, n_rep))
+        total = y[:rows]
+        for h in range(1, groups):
+            total = jnp.where(group == h, y[h * rows : (h + 1) * rows], total)
+        sign = (1 - 2 * rep_flip_ref[row, :]).astype(F32)
+        chosen.append((total * sign).astype(BF16))
+        w_sign = (1 - 2 * win_flip_ref[row, :]).astype(F32)
+        picks.append(jnp.where(m_own == win_pair_ref[row, :], w_sign, 0.0).astype(BF16))
+
+    def strings_tile(k):
+        base = k * WIDE
+        t = inner + base
+        s = lax.broadcasted_iota(jnp.int32, (WIDE, n_win), 0) + base
+        cols = pl.ds(pl.multiple_of(base, WIDE), WIDE)
+        for u, a in enumerate(strings):
+            row = pl.ds(a, 1)
+            store = pl.ds(pl.multiple_of(a * rows, rows), rows)
+            hit = jnp.where(t == rep_target_ref[row, :], 1.0, 0.0).astype(BF16)
+            reach = jnp.where(s == win_target_ref[row, :], 1.0, 0.0).astype(BF16)
+            g_ref[store, cols] = dot(chosen[u], hit, NT)
+            w_ref[store, cols] = dot(picks[u], reach, NT)
+
+    for_each(n_all // WIDE, strings_tile)
 
 
 def kernel(
     n_sig, n_xf,
+    coef_hbm, sym_alpha_hbm, sym_beta_hbm,
+    win_target_hbm, win_pair_hbm, win_flip_hbm,
+    rep_target_hbm, rep_pair_hbm, rep_flip_hbm,
+    half_hbm, orb_hbm, orb_sym_hbm, pair_sym_ref,
+    out_ref,
     coef_ref, sym_alpha_ref, sym_beta_ref,
     win_target_ref, win_pair_ref, win_flip_ref,
     rep_target_ref, rep_pair_ref, rep_flip_ref,
-    half_ref, orb_ref, orb_sym_ref, pair_sym_ref,
-    out_ref,
+    half_ref, orb_ref, orb_sym_ref,
     first_ref, block_ref, table_ref, g_ref, w_ref,
     c_ref, q_ref, q_in, p_ref, p_in, h_ref,
-    c_send, c_recv, q_send, q_recv, p_send, p_recv, h_send, h_recv,
+    c_send, c_recv, q_send, q_recv, p_send, p_recv, h_send, h_recv, load_sem,
 ):
     me = lax.axis_index("sig")
     own = lax.axis_index("xf")
     own_rows, n_beta = coef_ref.shape
-    n_orb = orb_ref.shape[1]
     n_all = own_rows * n_sig
     width = n_all // n_xf
 
+    pairs = (
+        (half_hbm, half_ref), (orb_hbm, orb_ref), (orb_sym_hbm, orb_sym_ref),
+        (coef_hbm, coef_ref), (sym_alpha_hbm, sym_alpha_ref), (sym_beta_hbm, sym_beta_ref),
+        (rep_pair_hbm, rep_pair_ref), (rep_target_hbm, rep_target_ref), (rep_flip_hbm, rep_flip_ref),
+        (win_target_hbm, win_target_ref), (win_pair_hbm, win_pair_ref), (win_flip_hbm, win_flip_ref),
+    )
+    loads = [pltpu.make_async_copy(src, dst, load_sem.at[k]) for k, (src, dst) in enumerate(pairs)]
+    for load in loads:
+        load.start()
+
     barrier = pltpu.get_barrier_semaphore()
 
     def greet_sig(k):
@@ -157,6 +158,8 @@
     for k in range(1, n_xf):
         greet_xf(k)
 
+    for load in loads[:6]:
+        load.wait()
     sym_alpha = column(sym_alpha_ref[...].reshape(1, own_rows), own_rows)
     sym_beta = sym_beta_ref[...].reshape(1, n_beta)
     allowed = jnp.bitwise_xor(sym_alpha, sym_beta) == 0
@@ -164,7 +167,6 @@
 
     transform(half_ref, orb_ref, orb_sym_ref, pair_sym_ref, first_ref, block_ref, table_ref)
 
-    pl.semaphore_wait(barrier, n_sig + n_xf - 2)
 
     def c_copy(k):
         return pltpu.make_async_remote_copy(
@@ -180,11 +182,16 @@
     def loop(low, high, step):
         lax.fori_loop(low, high, lambda k, _: (step(k), 0)[1], 0)
 
-    loop(1, n_sig, lambda k: c_copy(k).start())
-
+    for load in loads[6:]:
+        load.wait()
     win = (win_target_ref, win_pair_ref, win_flip_ref)
     rep = (rep_target_ref, rep_pair_ref, rep_flip_ref)
-    loop(0, own_rows, lambda a: couple(a, own, n_orb, win, rep, table_ref, g_ref, w_ref))
+    pl.semaphore_wait(barrier, n_sig + n_xf - 2)
+    loop(1, n_sig, lambda k: c_copy(k).start())
+    step = 4
+    loop(0, own_rows // step, lambda a: couple(
+        [a * step + u for u in range(step)], own, win, rep, table_ref, g_ref, w_ref))
+
 
     depth = g_ref.shape[0]
     tile = 256
@@ -272,21 +279,23 @@
     own_rows, n_beta = coef.shape
     rows = half_ints.shape[0]
     n_bas, n_orb = orbitals.shape
+    args = args[:10] + (orbitals.T,) + args[11:]
     n_all = own_rows * n_sig
     width = n_all // n_xf
-    half = n_orb * n_orb // LANES
+    groups = n_orb * n_orb // WIDE
     vmem = pl.BlockSpec(memory_space=pltpu.VMEM)
+    hbm = pl.BlockSpec(memory_space=pltpu.HBM)
     smem = pl.BlockSpec(memory_space=pltpu.SMEM)
     dma = pltpu.SemaphoreType.DMA
     return pl.pallas_call(
         functools.partial(kernel, n_sig, n_xf),
         out_shape=jax.ShapeDtypeStruct((own_rows, n_beta), F32),
-        in_specs=[vmem] * 12 + [smem],
+        in_specs=[hbm] * 12 + [smem],
         out_specs=vmem,
-        scratch_shapes=[
+        scratch_shapes=[pltpu.VMEM(arg.shape, arg.dtype) for arg in args[:12]] + [
             pltpu.VMEM((n_bas * rows, LANES), F32),
-            pltpu.VMEM((rows * half, LANES), F32),
-            pltpu.VMEM((rows * half, LANES), F32),
+            pltpu.VMEM((rows * n_orb, LANES), F32),
+            pltpu.VMEM((rows * groups, WIDE), BF16),
             pltpu.VMEM((own_rows * rows, n_all), F32),
             pltpu.VMEM((own_rows * rows, n_all), F32),
             pltpu.VMEM((n_sig, own_rows, n_beta), BF16),
@@ -299,9 +308,10 @@
             dma((n_xf - 1,)), dma((n_xf - 1,)),
             dma((n_sig,)), dma((n_sig,)),
             dma((n_xf - 1,)), dma((n_xf - 1,)),
+            dma((12,)),
         ],
         compiler_params=pltpu.CompilerParams(
-            collective_id=0, has_side_effects=True, vmem_limit_bytes=40 * 1024 * 1024
+            collective_id=0, has_side_effects=True, vmem_limit_bytes=60 * 1024 * 1024
         ),
     )(*args)
 

time: 35.7 us -> 19.6 us (0.55)
  Pallas kernels: 27.1 us -> 18.1 us
  local copies, waits for them, and re-layouts: 8.04 us -> 1.32 us
    pallas_call x1, Pallas kernels: 27.1 us -> 18.1 us  [body(): pl.pallas_call(functools.partial(kernel, n_sig, n_xf), out_shape=jax.Shap...]
    unnamed x26 -> x1, local copies, waits for them, and re-layouts: 8.04 us -> 1.32 us
where the time goes in v2:
time: 19.6 us; the launch traced here: 19.4 us
  Pallas kernels  18.1 us (92%)
  local copies, waits for them, and re-layouts  1.32 us (7%)
    pallas_call x1, Pallas kernels, body(): pl.pallas_call(functools.partial(kernel, n_sig, n_xf), out_shape=jax.Shap...  18.1 us
    unnamed x1, local copies, waits for them, and re-layouts  1.32 us

profile of v2, /device:TPU:0, one launch (start us, length us, event | category | flops | bytes accessed | tf_op | source)
XLA Modules:
  0.0 19.4 jit_solution(16130588289175965217)
XLA Ops:
  0.0 18.1 %shard_map.127 = f32[16,256]{1,0:T(8,128)} custom-call(bf16[16,256]{1,0:T(8,128)(2,1)} %coef_hbm.1, s32[16]{0:T(128)} %sym_alpha_hbm.1, s32[256]{0:T(256)} %sym_beta_hbm.1, s32[16,16]{1,0:T(8,128)} %win_target_hbm.1, s32[16,16]{1,0:T(8,128)} %win_pair_hbm.1, s32[16,16]{1,0:T(8,128)} %win_flip_hbm.1, s32[16,512]{1,0:T(8,128)} %rep_target_hbm.1, ...), custom_call_target="tpu_custom_call" | custom-call | tf_op jit(solution)/shard_map/pallas_call | solution.py:290
  18.1 1.3 %copy.15 = f32[16,256]{1,0:T(8,128)} copy(f32[16,256]{1,0:T(8,128)} %shard_map.127) | data formatting | bytes 32768

commit v3 on v2

--- a/solution.py
+++ b/solution.py
@@ -182,12 +182,16 @@
     def loop(low, high, step):
         lax.fori_loop(low, high, lambda k, _: (step(k), 0)[1], 0)
 
+    def each(low, high, step):
+        for k in range(low, high):
+            step(k)
+
     for load in loads[6:]:
         load.wait()
     win = (win_target_ref, win_pair_ref, win_flip_ref)
     rep = (rep_target_ref, rep_pair_ref, rep_flip_ref)
     pl.semaphore_wait(barrier, n_sig + n_xf - 2)
-    loop(1, n_sig, lambda k: c_copy(k).start())
+    each(1, n_sig, lambda k: c_copy(k).start())
     step = 4
     loop(0, own_rows // step, lambda a: couple(
         [a * step + u for u in range(step)], own, win, rep, table_ref, g_ref, w_ref))
@@ -212,7 +216,14 @@
             total = lax.fori_loop(0, depth // tile, part, jnp.zeros((tile, width), F32))
         q_ref[x, cols, :] = total
 
-    for_each(n_xf, lambda x: for_each(n_all // tile, lambda t: q_tile(t, x)))
+    if depth == tile and n_all == tile:
+        high, low = split(g_ref[...])
+        w = w_ref[...].astype(BF16)
+        total = dot(high, w, TN) + dot(low, w, TN)
+        for x in range(n_xf):
+            q_ref[x] = total[:, x * width : (x + 1) * width]
+    else:
+        for_each(n_xf, lambda x: for_each(n_all // tile, lambda t: q_tile(t, x)))
 
     def q_copy(k):
         there = lax.rem(own + k, n_xf)
@@ -241,9 +252,9 @@
             src_ref=p_ref.at[there], dst_ref=p_in.at[k], send_sem=p_send.at[k], recv_sem=p_recv.at[k],
             device_id=(there, own), device_id_type=MESH)
 
-    loop(1, n_sig, lambda k: p_copy(k).start())
+    each(1, n_sig, lambda k: p_copy(k).start())
     p_in[0] = p_ref[me]
-    loop(1, n_sig, lambda k: p_copy(k).wait_recv())
+    each(1, n_sig, lambda k: p_copy(k).wait_recv())
     h_ref[own] = jnp.sum(p_in[...].astype(F32), axis=0)
 
     def h_copy(k):
@@ -259,7 +270,7 @@
 
     for k in range(1, n_xf):
         h_copy(k).start()
-    loop(1, n_sig, lambda k: c_arrival(k).wait_recv())
+    each(1, n_sig, lambda k: c_arrival(k).wait_recv())
     for k in range(1, n_xf):
         h_arrival(k).wait_recv()
     high, low = split(jnp.concatenate([h_ref[x] for x in range(n_xf)], axis=1))
@@ -267,8 +278,8 @@
     total = dot(high, c_all, NN) + dot(low, c_all, NN)
     out_ref[...] = jnp.where(allowed, total, 0.0)
 
-    loop(1, n_sig, lambda k: c_copy(k).wait_send())
-    loop(1, n_sig, lambda k: p_copy(k).wait_send())
+    each(1, n_sig, lambda k: c_copy(k).wait_send())
+    each(1, n_sig, lambda k: p_copy(k).wait_send())
     for k in range(1, n_xf):
         q_copy(k).wait_send()
         h_copy(k).wait_send()

time: 19.6 us -> 19.3 us (0.985)
  Pallas kernels: 18.1 us -> 17.8 us
    pallas_call x1, Pallas kernels: 18.1 us -> 17.8 us  [body(): pl.pallas_call(functools.partial(kernel, n_sig, n_xf), out_shape=jax.Shap...]
where the time goes in v3:
time: 19.3 us; the launch traced here: 19.1 us
  Pallas kernels  17.8 us (92%)
  local copies, waits for them, and re-layouts  1.32 us (7%)
    pallas_call x1, Pallas kernels, body(): pl.pallas_call(functools.partial(kernel, n_sig, n_xf), out_shape=jax.Shap...  17.8 us
    unnamed x1, local copies, waits for them, and re-layouts  1.32 us

profile of v3, /device:TPU:0, one launch (start us, length us, event | category | flops | bytes accessed | tf_op | source)
XLA Modules:
  0.0 19.1 jit_solution(9529656678120533631)
XLA Ops:
  0.0 17.8 %shard_map.127 = f32[16,256]{1,0:T(8,128)} custom-call(bf16[16,256]{1,0:T(8,128)(2,1)} %coef_hbm.1, s32[16]{0:T(128)} %sym_alpha_hbm.1, s32[256]{0:T(256)} %sym_beta_hbm.1, s32[16,16]{1,0:T(8,128)} %win_target_hbm.1, s32[16,16]{1,0:T(8,128)} %win_pair_hbm.1, s32[16,16]{1,0:T(8,128)} %win_flip_hbm.1, s32[16,512]{1,0:T(8,128)} %rep_target_hbm.1, ...), custom_call_target="tpu_custom_call" | custom-call | tf_op jit(solution)/shard_map/pallas_call | solution.py:301
  17.8 1.3 %copy.15 = f32[16,256]{1,0:T(8,128)} copy(f32[16,256]{1,0:T(8,128)} %shard_map.127) | data formatting | bytes 32768
